TPU v7x, 128 devices: a whole 4x4x4 slice. The times are simulated.
128 devices in a mesh: blk: 16 (over x, y_lo, core), head: 8 (over y_hi, z).
Axes of the slice: x: 4, y: 4 (y_hi: 2, y_lo: 2; y = y_hi * 2 + y_lo), z: 4, core: 2. Of those that a mesh axis runs over, the one named last changes fastest.
Arguments:
- queries: bfloat16 [16384, 8192], P(('blk', 'head')), may hold values from -6 to 6
- keys: bfloat16 [16384, 1024], P(('blk', 'head')), may hold values from -6 to 6
- values: bfloat16 [16384, 1024], P(('blk', 'head')), may hold values from -6 to 6
- live_keys: int32 [16, 16, 16], replicated, may hold values from 0 to 63, as said below
- live_count: int32 [16, 16], replicated, may hold values from 1 to 16, as said below
Outputs:
- attended: bfloat16 [16384, 8192], P(('blk', 'head'))
Inputs may be any that keep to these rules, and one draw needn't show every extreme that they name: live_keys[i, j, c] = a * 8 + b names the pair (query block i * 8 + a, key block j * 8 + b); the codes of one (i, j) are distinct, and a == b never occurs for i == j. Only slots c < live_count[i, j] are live. `live_count`: for every query shard i, some key shard j has all 16 slots live.
All inputs are finite; a program needn't handle non-finite values.
Results may differ from a plain program's by a relative error of at most 0.0065.
Values may be sent and summed in bfloat16 or wider, within the bound.
No kernel may reach another device: no remote copies, remote signals or barrier semaphores. Data moves between devices by JAX's collectives and lax.ppermute only.
A program may use at most 128 MiB of HBM per device.

v0:
```python
import jax
import jax.numpy as jnp
from jax import lax
from jax.sharding import PartitionSpec as P

HEADS = 64
KV_HEADS = 8
HEAD_DIM = 128
BLOCK = 128


def add_tiles(carried, query_blocks, key_tiles, value_tiles, query_index, row_keep):
    running, denominator, weighted_sum = carried
    block_count = query_blocks.shape[0]
    query_tiles = jnp.take(query_blocks, query_index, axis=0)
    scores = jnp.einsum(
        "ctkgd,cukd->ckgtu", query_tiles, key_tiles, preferred_element_type=jnp.float32
    ) * HEAD_DIM ** (-0.5)
    scores = jnp.where(row_keep[:, None, None, None, :], scores, -jnp.inf)
    tile_live = jnp.any(row_keep, axis=1)
    one_hot = (
        query_index[:, None] == jnp.arange(block_count, dtype=jnp.int32)[None, :]
    ) & tile_live[:, None]
    tile_max = scores.max(-1)
    block_max = jnp.where(one_hot[:, :, None, None, None], tile_max[:, None], -jnp.inf).max(0)
    new_max = jnp.maximum(running, block_max)
    factor = jnp.exp(running - new_max)
    weights = jnp.exp(scores - jnp.take(new_max, query_index, axis=0)[..., None])
    hot_float = one_hot.astype(jnp.float32)
    denominator = denominator * factor + jnp.einsum(
        "cs,ckgt->skgt", hot_float, weights.sum(-1), precision=lax.Precision.HIGHEST
    )
    partial_sum = jnp.einsum(
        "ckgtu,cukd->ckgtd",
        weights.astype(jnp.bfloat16),
        value_tiles,
        preferred_element_type=jnp.float32,
    )
    weighted_sum = weighted_sum * factor[..., None]
    weighted_sum = weighted_sum + jnp.einsum(
        "cs,ckgtd->skgtd", hot_float, partial_sum, precision=lax.Precision.HIGHEST
    )
    return (new_max, denominator, weighted_sum)


def local(queries, keys, values, live_keys, live_count):
    query_local, key_local, value_local = (
        lax.all_to_all(queries, "head", split_axis=1, concat_axis=0, tiled=True),
        lax.all_to_all(keys, "head", split_axis=1, concat_axis=0, tiled=True),
        lax.all_to_all(values, "head", split_axis=1, concat_axis=0, tiled=True),
    )
    row_count = query_local.shape[0]
    block_count = row_count // BLOCK
    kv_local = key_local.shape[1] // HEAD_DIM
    group_count = HEADS // KV_HEADS
    query_blocks = query_local.reshape(block_count, BLOCK, kv_local, group_count, HEAD_DIM)
    key_blocks = key_local.reshape(block_count, BLOCK, kv_local, HEAD_DIM)
    value_blocks = value_local.reshape(block_count, BLOCK, kv_local, HEAD_DIM)
    my_shard = lax.axis_index("blk")
    cycle_size = lax.axis_size("blk")
    pair_codes = live_keys[my_shard]
    pair_counts = live_count[my_shard]
    slot_count = pair_codes.shape[1]
    slot_ids = jnp.arange(slot_count, dtype=jnp.int32)
    diagonal = jnp.einsum(
        "btkgd,bukd->bkgtu", query_blocks, key_blocks, preferred_element_type=jnp.float32
    ) * HEAD_DIM ** (-0.5)
    running = diagonal.max(-1)
    diag_weights = jnp.exp(diagonal - running[..., None])
    denominator = diag_weights.sum(-1)
    weighted_sum = jnp.einsum(
        "bkgtu,bukd->bkgtd",
        diag_weights.astype(jnp.bfloat16),
        value_blocks,
        preferred_element_type=jnp.float32,
    )
    carried = (running, denominator, weighted_sum)

    def fold_keys(carried, key_value):
        key_piece, value_piece = key_value
        piece_rows = key_piece.shape[0]
        piece_blocks = piece_rows // BLOCK
        key_piece_blocks = key_piece.reshape(piece_blocks, BLOCK, -1)
        value_piece_blocks = value_piece.reshape(piece_blocks, BLOCK, -1)
        touched = -(-piece_rows // row_count) + 0

        def visit_shard(offset, carried):
            in_range = offset < cycle_size
            kshard_clip = jnp.minimum(offset, cycle_size - 1)
            slot_codes = pair_codes[kshard_clip]
            slot_live = pair_counts[kshard_clip]
            tile_block = kshard_clip * block_count + slot_codes % block_count
            slot_keep = (
                (tile_block >= 0) & (tile_block < piece_blocks) & (slot_ids < slot_live) & in_range
            )
            row_keep = jnp.broadcast_to(slot_keep[:, None], (slot_count, BLOCK))
            tile_block = jnp.clip(tile_block, 0, piece_blocks - 1)
            key_tiles = jnp.take(key_piece_blocks, tile_block, axis=0).reshape(
                slot_count, BLOCK, kv_local, HEAD_DIM
            )
            value_tiles = jnp.take(value_piece_blocks, tile_block, axis=0).reshape(
                slot_count, BLOCK, kv_local, HEAD_DIM
            )
            return add_tiles(
                carried, query_blocks, key_tiles, value_tiles, slot_codes // block_count, row_keep
            )

        return lax.fori_loop(0, touched, visit_shard, carried)

    carried = fold_keys(
        carried,
        (
            lax.all_gather(key_local, "blk", axis=0, tiled=True),
            lax.all_gather(value_local, "blk", axis=0, tiled=True),
        ),
    )
    running, denominator, weighted_sum = carried
    normed = weighted_sum / denominator[..., None]
    normed = normed.astype(jnp.bfloat16).transpose(0, 3, 1, 2, 4).reshape(row_count, -1)
    return lax.all_to_all(normed, "head", split_axis=0, concat_axis=1, tiled=True)


def solution(mesh):
    return jax.shard_map(
        local,
        mesh=mesh,
        in_specs=(
            P(("blk", "head"), None),
            P(("blk", "head"), None),
            P(("blk", "head"), None),
            P(),
            P(),
        ),
        out_specs=P(("blk", "head"), None),
        check_vma=False,
    )
```

profile of v0, /device:TPU:1, one launch (start us, length us, event | category | flops | bytes accessed | tf_op | source)
XLA Modules:
  0.0 971.9 jit_solution(5417218941840749269)
XLA Ops:
  8.0 16.0 %all_to_all.73 = bf16[128,8,128]{2,0,1:T(8,128)(2,1)} all-to-all(bf16[128,8,128]{2,0,1:T(8,128)(2,1)S(1)} %copy.62), channel_id=1, replica_groups=mesh['blk'=16,'head'=8] {'head'}, dimensions={1} | all-to-all | bytes 524288 | tf_op jit(solution)/shard_map/all_to_all | solution.py:49
  25.4 10.8 %all_to_all.74 = bf16[128,8,128]{2,0,1:T(8,128)(2,1)} all-to-all(bf16[128,8,128]{2,0,1:T(8,128)(2,1)S(1)} %copy.66), channel_id=1, replica_groups=mesh['blk'=16,'head'=8] {'head'}, dimensions={1} | all-to-all | bytes 524288 | tf_op jit(solution)/shard_map/all_to_all | solution.py:50
  43.0 35.3 %all-to-all-done.1 = bf16[128,8,1024]{0,2,1:T(8,128)(2,1)S(1)} async-done(((bf16[128,8,1024]{0,2,1:T(8,128)(2,1)}), bf16[128,8,1024]{0,2,1:T(8,128)(2,1)S(1)}, u32[]{:S(2)}, u32[]{:S(2)}) %all-to-all-start.1) | async-done | bytes 2097184 | tf_op jit(solution)/shard_map/all_to_all | solution.py:48
  88.6 17.9 %all-gather.5.cloned.1.call-done = bf16[16384,128]{1,0:T(8,128)(2,1)} async-done(((bf16[1024,128]{1,0:T(8,128)(2,1)}), bf16[16384,128]{1,0:T(8,128)(2,1)}) %all-gather.5.cloned.1.call-update) | async-done | bytes 4194320 | tf_op jit(solution)/shard_map/all_gather | solution.py:114
  106.6 814.2 %while.20 = (s32[]{:T(128)}, f32[8,1,8,128]{3,0,2,1:T(8,128)S(1)}, f32[8,1,8,128]{3,0,2,1:T(8,128)S(1)}, f32[8,1,8,128,128]{4,0,3,2,1:T(8,128)}, s32[16,16]{1,0:...) while((s32[]{:T(128)}, f32[8,1,8,128]{3,0,2,1:T(8,128)S(1)}, ...), condition=%wide.region_7.9_spmd.clone, body=%wide.region_2.8_spmd.clone.sunk | while | flops 1304712960 | bytes 75638936 | solution.py:108
  144.1 13.3 %bitcast_add_fusion.2 = f32[8,1,8,128,128]{4,0,3,2,1:T(8,128)} fusion(f32[8,1,8,128,128]{4,0,3,2,1:T(8,128)} %get-tuple-element.437, f32[16,8,128,128]{3,2,1,0:T(8,128)} %fusion.76, f32[8,8,128]{0,2,1:T(8,128)S(1)} %copy.106, s32[16]{0:T(128)S(1)} %get-tuple-element.416, pred[16]{0:T(512)(128)(4,1)S(1)} %broadcast_reduce_fusion.2), kind=kOutput, calls=%fused_computation.15.clone.1 | convolution fusion | flops 203424000 | bytes 16810064 | tf_op jit(solution)/shard_map/while/body/eval_jaxpr/cs,ckgtd->skgtd/dot_general | solution.py:40
  195.0 13.3 %bitcast_add_fusion.2 = f32[8,1,8,128,128]{4,0,3,2,1:T(8,128)} fusion(f32[8,1,8,128,128]{4,0,3,2,1:T(8,128)} %get-tuple-element.437, f32[16,8,128,128]{3,2,1,0:T(8,128)} %fusion.76, f32[8,8,128]{0,2,1:T(8,128)S(1)} %copy.106, s32[16]{0:T(128)S(1)} %get-tuple-element.416, pred[16]{0:T(512)(128)(4,1)S(1)} %broadcast_reduce_fusion.2), kind=kOutput, calls=%fused_computation.15.clone.1 | convolution fusion | flops 203424000 | bytes 16810064 | tf_op jit(solution)/shard_map/while/body/eval_jaxpr/cs,ckgtd->skgtd/dot_general | solution.py:40
  245.9 13.3 %bitcast_add_fusion.2 = f32[8,1,8,128,128]{4,0,3,2,1:T(8,128)} fusion(f32[8,1,8,128,128]{4,0,3,2,1:T(8,128)} %get-tuple-element.437, f32[16,8,128,128]{3,2,1,0:T(8,128)} %fusion.76, f32[8,8,128]{0,2,1:T(8,128)S(1)} %copy.106, s32[16]{0:T(128)S(1)} %get-tuple-element.416, pred[16]{0:T(512)(128)(4,1)S(1)} %broadcast_reduce_fusion.2), kind=kOutput, calls=%fused_computation.15.clone.1 | convolution fusion | flops 203424000 | bytes 16810064 | tf_op jit(solution)/shard_map/while/body/eval_jaxpr/cs,ckgtd->skgtd/dot_general | solution.py:40
  296.8 13.3 %bitcast_add_fusion.2 = f32[8,1,8,128,128]{4,0,3,2,1:T(8,128)} fusion(f32[8,1,8,128,128]{4,0,3,2,1:T(8,128)} %get-tuple-element.437, f32[16,8,128,128]{3,2,1,0:T(8,128)} %fusion.76, f32[8,8,128]{0,2,1:T(8,128)S(1)} %copy.106, s32[16]{0:T(128)S(1)} %get-tuple-element.416, pred[16]{0:T(512)(128)(4,1)S(1)} %broadcast_reduce_fusion.2), kind=kOutput, calls=%fused_computation.15.clone.1 | convolution fusion | flops 203424000 | bytes 16810064 | tf_op jit(solution)/shard_map/while/body/eval_jaxpr/cs,ckgtd->skgtd/dot_general | solution.py:40
  347.7 13.3 %bitcast_add_fusion.2 = f32[8,1,8,128,128]{4,0,3,2,1:T(8,128)} fusion(f32[8,1,8,128,128]{4,0,3,2,1:T(8,128)} %get-tuple-element.437, f32[16,8,128,128]{3,2,1,0:T(8,128)} %fusion.76, f32[8,8,128]{0,2,1:T(8,128)S(1)} %copy.106, s32[16]{0:T(128)S(1)} %get-tuple-element.416, pred[16]{0:T(512)(128)(4,1)S(1)} %broadcast_reduce_fusion.2), kind=kOutput, calls=%fused_computation.15.clone.1 | convolution fusion | flops 203424000 | bytes 16810064 | tf_op jit(solution)/shard_map/while/body/eval_jaxpr/cs,ckgtd->skgtd/dot_general | solution.py:40
  398.6 13.3 %bitcast_add_fusion.2 = f32[8,1,8,128,128]{4,0,3,2,1:T(8,128)} fusion(f32[8,1,8,128,128]{4,0,3,2,1:T(8,128)} %get-tuple-element.437, f32[16,8,128,128]{3,2,1,0:T(8,128)} %fusion.76, f32[8,8,128]{0,2,1:T(8,128)S(1)} %copy.106, s32[16]{0:T(128)S(1)} %get-tuple-element.416, pred[16]{0:T(512)(128)(4,1)S(1)} %broadcast_reduce_fusion.2), kind=kOutput, calls=%fused_computation.15.clone.1 | convolution fusion | flops 203424000 | bytes 16810064 | tf_op jit(solution)/shard_map/while/body/eval_jaxpr/cs,ckgtd->skgtd/dot_general | solution.py:40
  449.5 13.3 %bitcast_add_fusion.2 = f32[8,1,8,128,128]{4,0,3,2,1:T(8,128)} fusion(f32[8,1,8,128,128]{4,0,3,2,1:T(8,128)} %get-tuple-element.437, f32[16,8,128,128]{3,2,1,0:T(8,128)} %fusion.76, f32[8,8,128]{0,2,1:T(8,128)S(1)} %copy.106, s32[16]{0:T(128)S(1)} %get-tuple-element.416, pred[16]{0:T(512)(128)(4,1)S(1)} %broadcast_reduce_fusion.2), kind=kOutput, calls=%fused_computation.15.clone.1 | convolution fusion | flops 203424000 | bytes 16810064 | tf_op jit(solution)/shard_map/while/body/eval_jaxpr/cs,ckgtd->skgtd/dot_general | solution.py:40
  500.3 13.3 %bitcast_add_fusion.2 = f32[8,1,8,128,128]{4,0,3,2,1:T(8,128)} fusion(f32[8,1,8,128,128]{4,0,3,2,1:T(8,128)} %get-tuple-element.437, f32[16,8,128,128]{3,2,1,0:T(8,128)} %fusion.76, f32[8,8,128]{0,2,1:T(8,128)S(1)} %copy.106, s32[16]{0:T(128)S(1)} %get-tuple-element.416, pred[16]{0:T(512)(128)(4,1)S(1)} %broadcast_reduce_fusion.2), kind=kOutput, calls=%fused_computation.15.clone.1 | convolution fusion | flops 203424000 | bytes 16810064 | tf_op jit(solution)/shard_map/while/body/eval_jaxpr/cs,ckgtd->skgtd/dot_general | solution.py:40
  551.2 13.3 %bitcast_add_fusion.2 = f32[8,1,8,128,128]{4,0,3,2,1:T(8,128)} fusion(f32[8,1,8,128,128]{4,0,3,2,1:T(8,128)} %get-tuple-element.437, f32[16,8,128,128]{3,2,1,0:T(8,128)} %fusion.76, f32[8,8,128]{0,2,1:T(8,128)S(1)} %copy.106, s32[16]{0:T(128)S(1)} %get-tuple-element.416, pred[16]{0:T(512)(128)(4,1)S(1)} %broadcast_reduce_fusion.2), kind=kOutput, calls=%fused_computation.15.clone.1 | convolution fusion | flops 203424000 | bytes 16810064 | tf_op jit(solution)/shard_map/while/body/eval_jaxpr/cs,ckgtd->skgtd/dot_general | solution.py:40
  602.1 13.3 %bitcast_add_fusion.2 = f32[8,1,8,128,128]{4,0,3,2,1:T(8,128)} fusion(f32[8,1,8,128,128]{4,0,3,2,1:T(8,128)} %get-tuple-element.437, f32[16,8,128,128]{3,2,1,0:T(8,128)} %fusion.76, f32[8,8,128]{0,2,1:T(8,128)S(1)} %copy.106, s32[16]{0:T(128)S(1)} %get-tuple-element.416, pred[16]{0:T(512)(128)(4,1)S(1)} %broadcast_reduce_fusion.2), kind=kOutput, calls=%fused_computation.15.clone.1 | convolution fusion | flops 203424000 | bytes 16810064 | tf_op jit(solution)/shard_map/while/body/eval_jaxpr/cs,ckgtd->skgtd/dot_general | solution.py:40
  644.0 8.8 fusion.76
  653.0 13.3 %bitcast_add_fusion.2 = f32[8,1,8,128,128]{4,0,3,2,1:T(8,128)} fusion(f32[8,1,8,128,128]{4,0,3,2,1:T(8,128)} %get-tuple-element.437, f32[16,8,128,128]{3,2,1,0:T(8,128)} %fusion.76, f32[8,8,128]{0,2,1:T(8,128)S(1)} %copy.106, s32[16]{0:T(128)S(1)} %get-tuple-element.416, pred[16]{0:T(512)(128)(4,1)S(1)} %broadcast_reduce_fusion.2), kind=kOutput, calls=%fused_computation.15.clone.1 | convolution fusion | flops 203424000 | bytes 16810064 | tf_op jit(solution)/shard_map/while/body/eval_jaxpr/cs,ckgtd->skgtd/dot_general | solution.py:40
  694.9 8.8 fusion.76
  703.9 13.3 %bitcast_add_fusion.2 = f32[8,1,8,128,128]{4,0,3,2,1:T(8,128)} fusion(f32[8,1,8,128,128]{4,0,3,2,1:T(8,128)} %get-tuple-element.437, f32[16,8,128,128]{3,2,1,0:T(8,128)} %fusion.76, f32[8,8,128]{0,2,1:T(8,128)S(1)} %copy.106, s32[16]{0:T(128)S(1)} %get-tuple-element.416, pred[16]{0:T(512)(128)(4,1)S(1)} %broadcast_reduce_fusion.2), kind=kOutput, calls=%fused_computation.15.clone.1 | convolution fusion | flops 203424000 | bytes 16810064 | tf_op jit(solution)/shard_map/while/body/eval_jaxpr/cs,ckgtd->skgtd/dot_general | solution.py:40
  754.8 13.3 %bitcast_add_fusion.2 = f32[8,1,8,128,128]{4,0,3,2,1:T(8,128)} fusion(f32[8,1,8,128,128]{4,0,3,2,1:T(8,128)} %get-tuple-element.437, f32[16,8,128,128]{3,2,1,0:T(8,128)} %fusion.76, f32[8,8,128]{0,2,1:T(8,128)S(1)} %copy.106, s32[16]{0:T(128)S(1)} %get-tuple-element.416, pred[16]{0:T(512)(128)(4,1)S(1)} %broadcast_reduce_fusion.2), kind=kOutput, calls=%fused_computation.15.clone.1 | convolution fusion | flops 203424000 | bytes 16810064 | tf_op jit(solution)/shard_map/while/body/eval_jaxpr/cs,ckgtd->skgtd/dot_general | solution.py:40
  805.7 13.3 %bitcast_add_fusion.2 = f32[8,1,8,128,128]{4,0,3,2,1:T(8,128)} fusion(f32[8,1,8,128,128]{4,0,3,2,1:T(8,128)} %get-tuple-element.437, f32[16,8,128,128]{3,2,1,0:T(8,128)} %fusion.76, f32[8,8,128]{0,2,1:T(8,128)S(1)} %copy.106, s32[16]{0:T(128)S(1)} %get-tuple-element.416, pred[16]{0:T(512)(128)(4,1)S(1)} %broadcast_reduce_fusion.2), kind=kOutput, calls=%fused_computation.15.clone.1 | convolution fusion | flops 203424000 | bytes 16810064 | tf_op jit(solution)/shard_map/while/body/eval_jaxpr/cs,ckgtd->skgtd/dot_general | solution.py:40
  856.6 13.3 %bitcast_add_fusion.2 = f32[8,1,8,128,128]{4,0,3,2,1:T(8,128)} fusion(f32[8,1,8,128,128]{4,0,3,2,1:T(8,128)} %get-tuple-element.437, f32[16,8,128,128]{3,2,1,0:T(8,128)} %fusion.76, f32[8,8,128]{0,2,1:T(8,128)S(1)} %copy.106, s32[16]{0:T(128)S(1)} %get-tuple-element.416, pred[16]{0:T(512)(128)(4,1)S(1)} %broadcast_reduce_fusion.2), kind=kOutput, calls=%fused_computation.15.clone.1 | convolution fusion | flops 203424000 | bytes 16810064 | tf_op jit(solution)/shard_map/while/body/eval_jaxpr/cs,ckgtd->skgtd/dot_general | solution.py:40
  907.5 13.3 %bitcast_add_fusion.2 = f32[8,1,8,128,128]{4,0,3,2,1:T(8,128)} fusion(f32[8,1,8,128,128]{4,0,3,2,1:T(8,128)} %get-tuple-element.437, f32[16,8,128,128]{3,2,1,0:T(8,128)} %fusion.76, f32[8,8,128]{0,2,1:T(8,128)S(1)} %copy.106, s32[16]{0:T(128)S(1)} %get-tuple-element.416, pred[16]{0:T(512)(128)(4,1)S(1)} %broadcast_reduce_fusion.2), kind=kOutput, calls=%fused_computation.15.clone.1 | convolution fusion | flops 203424000 | bytes 16810064 | tf_op jit(solution)/shard_map/while/body/eval_jaxpr/cs,ckgtd->skgtd/dot_general | solution.py:40
  929.0 33.2 %all_to_all.75 = bf16[8,128,1024]{1,2,0:T(8,128)(2,1)S(1)} all-to-all(bf16[8,128,1024]{1,2,0:T(8,128)(2,1)S(1)} %bitcast.192), channel_id=1, replica_groups=mesh['blk'=16,'head'=8] {'head'}, dimensions={0} | all-to-all | bytes 4194304 | tf_op jit(solution)/shard_map/all_to_all | solution.py:120
  (418 shorter events, 612.8 us)
Async XLA Ops:
  6.5 36.5 %copy-start = (s32[16,16,16]{2,1,0:T(8,128)S(1)}, s32[16,16,16]{2,1,0:T(8,128)}, u32[]{:S(2)}) copy-start(s32[16,16,16]{2,1,0:T(8,128)} %param.12) | copy-start | bytes 49156
  6.5 29.7 %copy-start.5 = (bf16[128,8192]{1,0:T(8,128)(2,1)S(1)}, bf16[128,8192]{1,0:T(8,128)(2,1)}, u32[]{:S(2)}) copy-start(bf16[128,8192]{1,0:T(8,128)(2,1)} %param.9) | copy-start | bytes 6291460
  6.5 82.1 %all-gather.3.cloned.1.call-start = ((), (), s32[]{:S(2)}) async-start(), calls=%async_computation.4 | async-start | bytes 4456448 | tf_op jit(solution)/shard_map/all_gather | solution.py:113
  24.0 82.5 %all-gather.5.cloned.1.call-start = ((), (), s32[]{:S(2)}) async-start(), calls=%async_computation.5 | async-start | bytes 4456448 | tf_op jit(solution)/shard_map/all_gather | solution.py:114
  36.2 42.1 %copy-start.3 = (bf16[128,8,128]{2,0,1:T(8,128)(2,1)S(1)}, bf16[128,8,128]{2,0,1:T(8,128)(2,1)}, u32[]{:S(2)}) copy-start(bf16[128,8,128]{2,0,1:T(8,128)(2,1)} %all_to_all.73) | copy-start | bytes 786436
  38.7 39.6 %all-to-all-start.1 = ((bf16[128,8,1024]{0,2,1:T(8,128)(2,1)}), bf16[128,8,1024]{0,2,1:T(8,128)(2,1)S(1)}, u32[]{:S(2)}, u32[]{:S(2)}) async-start(bf16[128,8,1024]{0,2,1:T(8,128)(2,1)} %bitcast.193), calls=%async_computation.1 | async-start | bytes 4194304 | tf_op jit(solution)/shard_map/all_to_all | solution.py:48
  78.3 1.7 copy-start.2
  78.3 1.7 copy-start.4
  929.0 36.1 %copy-start.1 = (s32[16,16,16]{2,1,0:T(8,128)S(1)}, s32[16,16,16]{2,1,0:T(8,128)}, u32[]{:S(2)}) copy-start(s32[16,16,16]{2,1,0:T(8,128)} %param.12) | copy-start | bytes 49156
Sparse Core Ops, SparseCore 0:
  24.1 44.4 all-gather.2
  70.3 36.1 all-gather.4
where the time goes:
time: 977 us; the launch traced here: 972 us
  matrix products  471 us (48%)
  other arithmetic  185 us (19%)
  local copies, waits for them, and re-layouts  184 us (19%)
  blocking collectives  60 us (6%)
  waiting for transfers between devices  53.3 us (5%)
  between operations  13.5 us (1%)
    dot_general x16, matrix products, add_tiles(): jnp.einsum('cs,ckgtd->skgtd', hot_float, partial_sum, precision=lax.Preci...  213 us
    dot_general x16, matrix products, add_tiles(): jnp.einsum('ckgtu,cukd->ckgtd', weights.astype(jnp.bfloat16), value_tiles...  141 us
    dot_general x16, matrix products, add_tiles(): jnp.einsum('ctkgd,cukd->ckgtu', query_tiles, key_tiles, preferred_element...  113 us
    reduce_sum x16, other arithmetic, add_tiles(): weights.sum(-1)  87.9 us
    select_n x32, other arithmetic, add_tiles(): query_tiles = jnp.take(query_blocks, query_index, axis=0)  73.7 us
    gather x16, local copies, waits for them, and re-layouts, add_tiles(): query_tiles = jnp.take(query_blocks, query_index, axis=0)  48.3 us
    gather x16, local copies, waits for them, and re-layouts, visit_shard(): jnp.take(value_piece_blocks, tile_block, axis=0)  45.4 us
    gather x16, local copies, waits for them, and re-layouts, visit_shard(): jnp.take(key_piece_blocks, tile_block, axis=0)  45.3 us
  transfers between devices with their start and end apart: 3, of which 2 were waited for; matrix products, arithmetic and copies ran while one was open for 2% of the time, Pallas kernels for 0%

commit v1 on v0

v1 whole, which is shorter than its diff:
```python
import functools

import jax
import jax.numpy as jnp
from jax import lax
from jax.experimental import pallas as pl
from jax.experimental.pallas import tpu as pltpu
from jax.sharding import PartitionSpec as P

HEADS = 64
KV_HEADS = 8
HEAD_DIM = 128
BLOCK = 128
LOG2E = 1.4426950408889634
CHUNK = 8
ROW_HEADS = 2


def plan_kernel(shard_ref, codes_ref, counts_ref, key_ref, value_ref, chunks_ref, fill_ref, *, blocks, shards, zero):
    shard = shard_ref[0]
    for a in range(blocks):
        own = shard * blocks + a
        key_ref[a, 0] = own
        value_ref[a, 0] = own
        fill_ref[a] = 1

    def visit_shard(j, _):
        def visit_slot(c, _):
            code = codes_ref[shard, j, c]
            a = lax.div(code, blocks)
            block = j * blocks + lax.rem(code, blocks)
            at = fill_ref[a]
            key_ref[a, at] = block
            value_ref[a, at] = block
            fill_ref[a] = at + 1
            return 0

        return lax.fori_loop(0, counts_ref[shard, j], visit_slot, 0)

    lax.fori_loop(0, shards, visit_shard, 0)
    for a in range(blocks):
        own = shard * blocks + a
        filled = fill_ref[a]
        chunks = lax.div(filled + CHUNK - 1, CHUNK)
        chunks_ref[a] = chunks

        def pad(at, _):
            key_ref[a, at] = own
            value_ref[a, at] = zero
            return 0

        lax.fori_loop(filled, chunks * CHUNK, pad, 0)


def plan(shard, live_keys, live_count, blocks, zero):
    shards = live_keys.shape[0]
    width = -(-(shards * blocks + 1) // CHUNK) * CHUNK
    smem = pl.BlockSpec(memory_space=pltpu.SMEM)
    return pl.pallas_call(
        functools.partial(plan_kernel, blocks=blocks, shards=shards, zero=zero),
        in_specs=[smem] * 3,
        out_specs=[smem] * 3,
        out_shape=[
            jax.ShapeDtypeStruct((blocks, width), jnp.int32),
            jax.ShapeDtypeStruct((blocks, width), jnp.int32),
            jax.ShapeDtypeStruct((blocks,), jnp.int32),
        ],
        scratch_shapes=[pltpu.SMEM((blocks,), jnp.int32)],
    )(shard[None].astype(jnp.int32), live_keys, live_count)


def attend_kernel(
    key_at, value_at, chunks, queries, keys_hbm, values_hbm, out, keys, values, total, peak, sem, *, heads
):
    b = pl.program_id(0)
    count = keys.shape[0]

    @pl.when(b == 0)
    def _():
        key_copy = pltpu.make_async_copy(keys_hbm, keys, sem.at[0])
        value_copy = pltpu.make_async_copy(
            values_hbm, values.at[pl.ds(0, count), :, pl.ds(0, HEAD_DIM)], sem.at[1]
        )
        key_copy.start()
        value_copy.start()
        values[pl.ds(0, count), :, pl.ds(HEAD_DIM, HEAD_DIM)] = jnp.ones(
            (count, BLOCK, HEAD_DIM), jnp.bfloat16
        )
        values[count] = jnp.zeros((BLOCK, 2 * HEAD_DIM), jnp.bfloat16)
        key_copy.wait()
        value_copy.wait()

    total[...] = jnp.zeros(total.shape, jnp.float32)
    peak[...] = jnp.full(peak.shape, -jnp.inf, jnp.float32)

    def visit(i, _):
        key_tile = jnp.concatenate([keys[key_at[b, i * CHUNK + c]] for c in range(CHUNK)], axis=0)
        value_tile = jnp.concatenate([values[value_at[b, i * CHUNK + c]] for c in range(CHUNK)], axis=0)
        for first in range(0, heads, ROW_HEADS):
            rows = slice(first * BLOCK, (first + ROW_HEADS) * BLOCK)
            query_tile = jnp.concatenate(
                [queries[:, h * HEAD_DIM : (h + 1) * HEAD_DIM] for h in range(first, first + ROW_HEADS)],
                axis=0,
            )
            scores = lax.dot_general(
                query_tile, key_tile, (((1,), (1,)), ((), ())), preferred_element_type=jnp.float32
            ) * (HEAD_DIM**-0.5 * LOG2E)
            old = peak[rows, :]
            new = jnp.maximum(old, jnp.max(scores, axis=1, keepdims=True))
            factor = jnp.exp2(old - new)
            weights = jnp.exp2(scores - jnp.concatenate([new] * CHUNK, axis=1)).astype(jnp.bfloat16)
            part = jnp.dot(weights, value_tile, preferred_element_type=jnp.float32)
            total[rows, :] = total[rows, :] * jnp.concatenate([factor, factor], axis=1) + part
            peak[rows, :] = new
        return 0

    lax.fori_loop(0, chunks[b], visit, 0)
    for h in range(heads):
        rows = total[h * BLOCK : (h + 1) * BLOCK, :]
        out[:, h * HEAD_DIM : (h + 1) * HEAD_DIM] = (rows[:, :HEAD_DIM] / rows[:, HEAD_DIM:]).astype(
            jnp.bfloat16
        )


def attend(queries, keys, values, lists):
    rows, width = queries.shape
    heads = width // HEAD_DIM
    count = keys.shape[0]
    return pl.pallas_call(
        functools.partial(attend_kernel, heads=heads),
        grid_spec=pltpu.PrefetchScalarGridSpec(
            num_scalar_prefetch=3,
            grid=(rows // BLOCK,),
            in_specs=[
                pl.BlockSpec((BLOCK, width), lambda b, *_: (b, 0)),
                pl.BlockSpec(memory_space=pl.ANY),
                pl.BlockSpec(memory_space=pl.ANY),
            ],
            out_specs=pl.BlockSpec((BLOCK, width), lambda b, *_: (b, 0)),
            scratch_shapes=[
                pltpu.VMEM((count, BLOCK, HEAD_DIM), jnp.bfloat16),
                pltpu.VMEM((count + 1, BLOCK, 2 * HEAD_DIM), jnp.bfloat16),
                pltpu.VMEM((heads * BLOCK, 2 * HEAD_DIM), jnp.float32),
                pltpu.VMEM((heads * BLOCK, HEAD_DIM), jnp.float32),
                pltpu.SemaphoreType.DMA((2,)),
            ],
        ),
        out_shape=jax.ShapeDtypeStruct((rows, width), jnp.bfloat16),
        compiler_params=pltpu.CompilerParams(vmem_limit_bytes=48 * 1024 * 1024),
    )(*lists, queries, keys, values)


def local(queries, keys, values, live_keys, live_count):
    parts = lax.axis_size("head")
    tokens = queries.shape[0]

    def spread(array):
        cut = array.reshape(tokens, parts, -1).transpose(1, 0, 2)
        moved = lax.all_to_all(cut, "head", split_axis=0, concat_axis=0, tiled=True)
        return moved.reshape(parts * tokens, -1)

    key_value = jnp.concatenate(
        [keys.reshape(tokens, parts, -1), values.reshape(tokens, parts, -1)], axis=2
    )
    key_value = spread(key_value)
    width = key_value.shape[1] // 2
    key_all = lax.all_gather(key_value[:, :width], "blk", axis=0, tiled=True)
    value_all = lax.all_gather(key_value[:, width:], "blk", axis=0, tiled=True)
    query_local = spread(queries)
    blocks = query_local.shape[0] // BLOCK
    count = key_all.shape[0] // BLOCK
    lists = plan(lax.axis_index("blk"), live_keys, live_count, blocks, count)
    attended = attend(
        query_local,
        key_all.reshape(count, BLOCK, -1),
        value_all.reshape(count, BLOCK, -1),
        lists,
    )
    back = lax.all_to_all(
        attended.reshape(parts, tokens, -1), "head", split_axis=0, concat_axis=0, tiled=True
    )
    return back.transpose(1, 0, 2).reshape(tokens, -1)


def solution(mesh):
    return jax.shard_map(
        local,
        mesh=mesh,
        in_specs=(
            P(("blk", "head"), None),
            P(("blk", "head"), None),
            P(("blk", "head"), None),
            P(),
            P(),
        ),
        out_specs=P(("blk", "head"), None),
        check_vma=False,
    )
```

time: 977 us -> 212 us (0.22)
  matrix products: 471 us -> 0 us
  other arithmetic: 185 us -> 0.04 us
  local copies, waits for them, and re-layouts: 184 us -> 8.37 us
  Pallas kernels: 0 us -> 56.2 us
  waiting for transfers between devices: 53.3 us -> 77.9 us
    dot_general x66 -> x0, matrix products: 471 us -> none  [the longest x16 213 us: add_tiles(): jnp.einsum('cs,ckgtd->skgtd', hot_float, partial_sum, precision=lax.Preci...]
    gather x64 -> x0, local copies, waits for them, and re-layouts: 148 us -> none  [the longest x16 48.3 us: add_tiles(): query_tiles = jnp.take(query_blocks, query_index, axis=0)]
    reduce_sum x17 -> x0, other arithmetic: 88.9 us -> none  [the longest x16 87.9 us: add_tiles(): weights.sum(-1)]
    select_n x48 -> x0, other arithmetic: 75 us -> none  [the longest x32 73.7 us: add_tiles(): query_tiles = jnp.take(query_blocks, query_index, axis=0)]
    pallas_call x0 -> x2, Pallas kernels: none -> 56.2 us  [the longest x1 48.6 us: attend(): pl.pallas_call(functools.partial(attend_kernel, heads=heads), grid_spec=p...]
    all_gather x2, waiting for transfers between devices: 18 us -> 41.3 us  [the longest x1 40.4 us: local(): value_all = lax.all_gather(key_value[:, width:], 'blk', axis=0, tiled=True)]
    and x48 -> x0, other arithmetic: 11.1 us -> none  [the longest x16 10.6 us: visit_shard(): (tile_block >= 0) & (tile_block < piece_blocks) & (slot_ids < slot_live)]
    all_to_all x3 -> x2, blocking collectives: 60 us -> 51.5 us  [the longest x1 33.1 us: local(): lax.all_to_all(attended.reshape(parts, tokens, -1), 'head', split_axis=0,...]
  transfers between devices with their start and end apart: 3 -> 3, of which waited for: 2 -> 3; matrix products, arithmetic and copies ran while one was open for 2% -> 1% of each run, Pallas kernels for 0% -> 4%
where the time goes in v1:
time: 212 us; the launch traced here: 211 us
  waiting for transfers between devices  77.9 us (37%)
  Pallas kernels  56.2 us (27%)
  blocking collectives  51.5 us (24%)
  between operations  13.5 us (6%)
  local copies, waits for them, and re-layouts  8.37 us (4%)
  starting transfers between devices  3.65 us (2%)
    pallas_call x1, Pallas kernels, attend(): pl.pallas_call(functools.partial(attend_kernel, heads=heads), grid_spec=p...  48.6 us
    all_gather x1, waiting for transfers between devices, local(): value_all = lax.all_gather(key_value[:, width:], 'blk', axis=0, tiled=True)  40.4 us
    all_to_all x1, waiting for transfers between devices, spread(): moved = lax.all_to_all(cut, 'head', split_axis=0, concat_axis=0, tiled=True)  35.9 us
    all_to_all x1, blocking collectives, local(): lax.all_to_all(attended.reshape(parts, tokens, -1), 'head', split_axis=0,...  33.1 us
    all_to_all x1, blocking collectives, spread(): moved = lax.all_to_all(cut, 'head', split_axis=0, concat_axis=0, tiled=True)  18.4 us
    pallas_call x1, Pallas kernels, plan(): pl.pallas_call(functools.partial(plan_kernel, blocks=blocks, shards=shard...  7.54 us
    unnamed x10, local copies, waits for them, and re-layouts  4.24 us
  transfers between devices with their start and end apart: 3, of which 3 were waited for; matrix products, arithmetic and copies ran while one was open for 1% of the time, Pallas kernels for 4%

profile of v1, /device:TPU:1, one launch (start us, length us, event | category | flops | bytes accessed | tf_op | source)
XLA Modules:
  0.0 211.1 jit_solution(11421749175633150484)
XLA Ops:
  6.5 0.0 all-gather.3.cloned.1.call-start
  6.5 1.1 copy.13
  7.7 1.1 copy.12
  8.8 0.0 copy-start.3
  8.8 0.2 copy.14
  9.1 18.4 %all_to_all.15 = bf16[8,128,256]{2,1,0:T(8,128)(2,1)S(1)} all-to-all(bf16[8,128,256]{2,1,0:T(8,128)(2,1)S(1)} %copy.14), channel_id=1, replica_groups=mesh['blk'=16,'head'=8] {'head'}, dimensions={0} | all-to-all | bytes 1048576 | tf_op jit(solution)/shard_map/all_to_all | solution.py:159
  27.5 0.9 fusion
  28.3 0.0 all-gather.3.cloned.1.call-update
  28.4 0.0 all-gather.5.cloned.1.call-start
  28.4 0.7 all-gather.5.cloned.1.call-update
  29.1 0.0 copy-done.3
  29.1 1.6 copy.19
  30.7 3.6 %all-to-all-start = ((bf16[8,128,1024]{2,1,0:T(8,128)(2,1)}), bf16[8,128,1024]{2,1,0:T(8,128)(2,1)S(1)}, u32[]{:S(2)}, u32[]{:S(2)}) async-start(bf16[8,128,1024]{2,1,0:T(8,128)(2,1)} %bitcast.22), calls=%async_computation | async-start | bytes 4194304 | tf_op jit(solution)/shard_map/all_to_all | solution.py:159
  34.3 7.5 %shard_map.55 = (s32[8,136]{1,0:T(8,128)}, s32[8,136]{1,0:T(8,128)}, s32[8]{0:T(128)}) custom-call(s32[1]{0:T(128)} %bitcast.shard_ref, s32[16,16,16]{2,1,0:T(8,128)} %codes_ref.1, s32[16,16]{1,0:T(8,128)} %counts_ref.1), custom_call_target="tpu_custom_call" | custom-call | tf_op jit(solution)/shard_map/pallas_call | solution.py:59
  41.8 35.9 %all-to-all-done = bf16[8,128,1024]{2,1,0:T(8,128)(2,1)S(1)} async-done(((bf16[8,128,1024]{2,1,0:T(8,128)(2,1)}), bf16[8,128,1024]{2,1,0:T(8,128)(2,1)S(1)}, u32[]{:S(2)}, u32[]{:S(2)}) %all-to-all-start) | async-done | bytes 2097184 | tf_op jit(solution)/shard_map/all_to_all | solution.py:159
  77.7 0.9 all-gather.3.cloned.1.call-done
  78.6 40.4 %all-gather.5.cloned.1.call-done = bf16[16384,128]{1,0:T(8,128)(2,1)} async-done(((bf16[1024,128]{1,0:T(8,128)(2,1)}), bf16[16384,128]{1,0:T(8,128)(2,1)}) %all-gather.5.cloned.1.call-update) | async-done | bytes 4194320 | tf_op jit(solution)/shard_map/all_gather | solution.py:168
  119.0 0.0 copy-start
  119.0 0.7 copy-done
  119.7 0.7 copy-done.1
  120.4 0.6 copy-done.2
  121.0 48.6 %shard_map.56 = bf16[1024,1024]{1,0:T(8,128)(2,1)S(1)} custom-call(s32[8,136]{1,0:T(8,128)S(1)} %copy-done, s32[8,136]{1,0:T(8,128)S(1)} %copy-done.1, s32[8]{0:T(128)S(1)} %copy-done.2, bf16[1024,1024]{1,0:T(8,128)(2,1)S(1)} %bitcast.20, bf16[128,128,128]{2,1,0:T(8,128)(2,1)} %bitcast.24, bf16[128,128,128]{2,1,0:T(8,128)(2,1)} %bitcast.25), custom_call_target="tpu_custom_call" | custom-call | tf_op jit(solution)/shard_map/pallas_call | solution.py:129
  169.7 33.1 %all_to_all.16 = bf16[8,128,1024]{2,1,0:T(8,128)(2,1)S(1)} all-to-all(bf16[8,128,1024]{2,1,0:T(8,128)(2,1)S(1)} %bitcast.21), channel_id=1, replica_groups=mesh['blk'=16,'head'=8] {'head'}, dimensions={0} | all-to-all | bytes 4194304 | tf_op jit(solution)/shard_map/all_to_all | solution.py:179
  202.8 1.5 copy.17
  (3 shorter events, 0.0 us)
Async XLA Ops:
  6.5 72.1 %all-gather.3.cloned.1.call-start = ((), (), s32[]{:S(2)}) async-start(), calls=%async_computation.3 | async-start | bytes 4456448 | tf_op jit(solution)/shard_map/all_gather | solution.py:167
  8.8 20.3 %copy-start.3 = (bf16[128,8192]{1,0:T(8,128)(2,1)S(1)}, bf16[128,8192]{1,0:T(8,128)(2,1)}, u32[]{:S(2)}) copy-start(bf16[128,8192]{1,0:T(8,128)(2,1)} %param.5) | copy-start | bytes 6291460
  28.4 90.7 %all-gather.5.cloned.1.call-start = ((), (), s32[]{:S(2)}) async-start(), calls=%async_computation.4 | async-start | bytes 4456448 | tf_op jit(solution)/shard_map/all_gather | solution.py:168
  30.7 47.0 %all-to-all-start = ((bf16[8,128,1024]{2,1,0:T(8,128)(2,1)}), bf16[8,128,1024]{2,1,0:T(8,128)(2,1)S(1)}, u32[]{:S(2)}, u32[]{:S(2)}) async-start(bf16[8,128,1024]{2,1,0:T(8,128)(2,1)} %bitcast.22), calls=%async_computation | async-start | bytes 4194304 | tf_op jit(solution)/shard_map/all_to_all | solution.py:159
  119.0 0.7 copy-start
  119.7 0.7 copy-start.1
  120.4 0.6 copy-start.2
Sparse Core Ops, SparseCore 0:
  28.5 50.0 all-gather.2
  80.3 38.6 all-gather.4

commit v2 on v1

--- a/solution.py
+++ b/solution.py
@@ -14,25 +14,29 @@
 LOG2E = 1.4426950408889634
 CHUNK = 8
 ROW_HEADS = 2
+HEAD_PARTS = 2
 
 
 def plan_kernel(shard_ref, codes_ref, counts_ref, key_ref, value_ref, chunks_ref, fill_ref, *, blocks, shards, zero):
     shard = shard_ref[0]
     for a in range(blocks):
-        own = shard * blocks + a
-        key_ref[a, 0] = own
-        value_ref[a, 0] = own
-        fill_ref[a] = 1
+        fill_ref[a] = 0
+
+    def append(a, block):
+        at = fill_ref[a]
+        key_ref[a, at] = block
+        value_ref[a, at] = block
+        fill_ref[a] = at + 1
 
     def visit_shard(j, _):
+        @pl.when(j == shard)
+        def _():
+            for a in range(blocks):
+                append(a, shard * blocks + a)
+
         def visit_slot(c, _):
             code = codes_ref[shard, j, c]
-            a = lax.div(code, blocks)
-            block = j * blocks + lax.rem(code, blocks)
-            at = fill_ref[a]
-            key_ref[a, at] = block
-            value_ref[a, at] = block
-            fill_ref[a] = at + 1
+            append(lax.div(code, blocks), j * blocks + lax.rem(code, blocks))
             return 0
 
         return lax.fori_loop(0, counts_ref[shard, j], visit_slot, 0)
@@ -66,36 +70,60 @@
             jax.ShapeDtypeStruct((blocks,), jnp.int32),
         ],
         scratch_shapes=[pltpu.SMEM((blocks,), jnp.int32)],
+        cost_estimate=pl.CostEstimate(flops=0, bytes_accessed=20_000_000, transcendentals=0),
     )(shard[None].astype(jnp.int32), live_keys, live_count)
 
 
 def attend_kernel(
-    key_at, value_at, chunks, queries, keys_hbm, values_hbm, out, keys, values, total, peak, sem, *, heads
+    key_at, value_at, chunks, queries, gathered, out, pairs, ones, total, peak, ready, sem, *, heads, shards
 ):
     b = pl.program_id(0)
-    count = keys.shape[0]
+    count = pairs.shape[0] - 1
+    span = count // shards
+
+    def arrival(j):
+        part = pl.ds(j * span, span)
+        return pltpu.make_async_copy(gathered.at[part], pairs.at[part], sem.at[j])
 
     @pl.when(b == 0)
     def _():
-        key_copy = pltpu.make_async_copy(keys_hbm, keys, sem.at[0])
-        value_copy = pltpu.make_async_copy(
-            values_hbm, values.at[pl.ds(0, count), :, pl.ds(0, HEAD_DIM)], sem.at[1]
-        )
-        key_copy.start()
-        value_copy.start()
-        values[pl.ds(0, count), :, pl.ds(HEAD_DIM, HEAD_DIM)] = jnp.ones(
-            (count, BLOCK, HEAD_DIM), jnp.bfloat16
-        )
-        values[count] = jnp.zeros((BLOCK, 2 * HEAD_DIM), jnp.bfloat16)
-        key_copy.wait()
-        value_copy.wait()
+        def begin(j, _):
+            arrival(j).start()
+            return 0
+
+        lax.fori_loop(0, shards, begin, 0)
+        ready[0] = 0
+        ones[0] = jnp.ones(ones.shape[1:], jnp.bfloat16)
+        ones[1] = jnp.zeros(ones.shape[1:], jnp.bfloat16)
+        pairs[count] = jnp.zeros(pairs.shape[1:], jnp.bfloat16)
 
     total[...] = jnp.zeros(total.shape, jnp.float32)
     peak[...] = jnp.full(peak.shape, -jnp.inf, jnp.float32)
 
     def visit(i, _):
-        key_tile = jnp.concatenate([keys[key_at[b, i * CHUNK + c]] for c in range(CHUNK)], axis=0)
-        value_tile = jnp.concatenate([values[value_at[b, i * CHUNK + c]] for c in range(CHUNK)], axis=0)
+        @pl.when(b == 0)
+        def _():
+            last = lax.div(key_at[b, i * CHUNK + CHUNK - 1], span) + 1
+            needed = jnp.where(i == chunks[b] - 1, shards, last)
+
+            def finish(j, _):
+                arrival(j).wait()
+                return 0
+
+            lax.fori_loop(ready[0], needed, finish, 0)
+            ready[0] = jnp.maximum(ready[0], needed)
+
+        key_tile = jnp.concatenate(
+            [pairs[key_at[b, i * CHUNK + c], :, :HEAD_DIM] for c in range(CHUNK)], axis=0
+        )
+        slots = [value_at[b, i * CHUNK + c] for c in range(CHUNK)]
+        value_tile = jnp.concatenate(
+            [
+                jnp.concatenate([pairs[s, :, HEAD_DIM:] for s in slots], axis=0),
+                jnp.concatenate([ones[(s == count).astype(jnp.int32)] for s in slots], axis=0),
+            ],
+            axis=1,
+        )
         for first in range(0, heads, ROW_HEADS):
             rows = slice(first * BLOCK, (first + ROW_HEADS) * BLOCK)
             query_tile = jnp.concatenate(
@@ -122,32 +150,35 @@
         )
 
 
-def attend(queries, keys, values, lists):
-    rows, width = queries.shape
+def attend(queries, gathered, lists, shards, part, parts):
+    rows, all_width = queries.shape
+    width = all_width // parts
     heads = width // HEAD_DIM
-    count = keys.shape[0]
+    count = gathered.shape[0]
+    pair_estimate = 180 * 2 * 2 * heads * BLOCK * BLOCK * HEAD_DIM
     return pl.pallas_call(
-        functools.partial(attend_kernel, heads=heads),
+        functools.partial(attend_kernel, heads=heads, shards=shards),
         grid_spec=pltpu.PrefetchScalarGridSpec(
             num_scalar_prefetch=3,
             grid=(rows // BLOCK,),
             in_specs=[
-                pl.BlockSpec((BLOCK, width), lambda b, *_: (b, 0)),
-                pl.BlockSpec(memory_space=pl.ANY),
+                pl.BlockSpec((BLOCK, width), lambda b, *_: (b, part)),
                 pl.BlockSpec(memory_space=pl.ANY),
             ],
             out_specs=pl.BlockSpec((BLOCK, width), lambda b, *_: (b, 0)),
             scratch_shapes=[
-                pltpu.VMEM((count, BLOCK, HEAD_DIM), jnp.bfloat16),
                 pltpu.VMEM((count + 1, BLOCK, 2 * HEAD_DIM), jnp.bfloat16),
+                pltpu.VMEM((2, BLOCK, HEAD_DIM), jnp.bfloat16),
                 pltpu.VMEM((heads * BLOCK, 2 * HEAD_DIM), jnp.float32),
                 pltpu.VMEM((heads * BLOCK, HEAD_DIM), jnp.float32),
-                pltpu.SemaphoreType.DMA((2,)),
+                pltpu.SMEM((1,), jnp.int32),
+                pltpu.SemaphoreType.DMA((shards,)),
             ],
         ),
         out_shape=jax.ShapeDtypeStruct((rows, width), jnp.bfloat16),
         compiler_params=pltpu.CompilerParams(vmem_limit_bytes=48 * 1024 * 1024),
-    )(*lists, queries, keys, values)
+        cost_estimate=pl.CostEstimate(flops=pair_estimate * 3, bytes_accessed=12_000_000, transcendentals=0),
+    )(*lists, queries, gathered)
 
 
 def local(queries, keys, values, live_keys, live_count):
@@ -159,26 +190,24 @@
         moved = lax.all_to_all(cut, "head", split_axis=0, concat_axis=0, tiled=True)
         return moved.reshape(parts * tokens, -1)
 
-    key_value = jnp.concatenate(
-        [keys.reshape(tokens, parts, -1), values.reshape(tokens, parts, -1)], axis=2
+    key_value = spread(
+        jnp.concatenate([keys.reshape(tokens, parts, -1), values.reshape(tokens, parts, -1)], axis=2)
     )
-    key_value = spread(key_value)
-    width = key_value.shape[1] // 2
-    key_all = lax.all_gather(key_value[:, :width], "blk", axis=0, tiled=True)
-    value_all = lax.all_gather(key_value[:, width:], "blk", axis=0, tiled=True)
+    gathered = lax.all_gather(key_value, "blk", axis=0, tiled=True)
     query_local = spread(queries)
     blocks = query_local.shape[0] // BLOCK
-    count = key_all.shape[0] // BLOCK
+    count = gathered.shape[0] // BLOCK
     lists = plan(lax.axis_index("blk"), live_keys, live_count, blocks, count)
-    attended = attend(
-        query_local,
-        key_all.reshape(count, BLOCK, -1),
-        value_all.reshape(count, BLOCK, -1),
-        lists,
-    )
-    back = lax.all_to_all(
-        attended.reshape(parts, tokens, -1), "head", split_axis=0, concat_axis=0, tiled=True
-    )
+    gathered = gathered.reshape(count, BLOCK, -1)
+    backs = []
+    for part in range(HEAD_PARTS):
+        attended = attend(query_local, gathered, lists, live_keys.shape[0], part, HEAD_PARTS)
+        backs.append(
+            lax.all_to_all(
+                attended.reshape(parts, tokens, -1), "head", split_axis=0, concat_axis=0, tiled=True
+            )
+        )
+    back = jnp.concatenate(backs, axis=2)
     return back.transpose(1, 0, 2).reshape(tokens, -1)
 
 

time: 212 us -> 207 us (0.976)
  the two profiles are of different devices: /device:TPU:1 before, /device:TPU:12 now
where the time goes in v2:
time: 207 us; the launch traced here: 203 us
  Pallas kernels  77.7 us (38%)
  waiting for transfers between devices  54 us (26%)
  blocking collectives  38.4 us (19%)
  between operations  13.5 us (7%)
  starting transfers between devices  9.92 us (5%)
  local copies, waits for them, and re-layouts  7.75 us (4%)
    pallas_call x2, Pallas kernels, attend(): pl.pallas_call(functools.partial(attend_kernel, heads=heads, shards=shard...  69.5 us
    all_gather x1, waiting for transfers between devices, local(): gathered = lax.all_gather(key_value, 'blk', axis=0, tiled=True)  37.5 us
    all_to_all x1, blocking collectives, local(): lax.all_to_all(attended.reshape(parts, tokens, -1), 'head', split_axis=0,...  19.9 us
    all_to_all x1, blocking collectives, spread(): moved = lax.all_to_all(cut, 'head', split_axis=0, concat_axis=0, tiled=True)  18.5 us
    all_to_all x1, waiting for transfers between devices, spread(): moved = lax.all_to_all(cut, 'head', split_axis=0, concat_axis=0, tiled=True)  16.5 us
    pallas_call x1, Pallas kernels, plan(): pl.pallas_call(functools.partial(plan_kernel, blocks=blocks, shards=shard...  8.21 us
    all_to_all x1, starting transfers between devices, local(): lax.all_to_all(attended.reshape(parts, tokens, -1), 'head', split_axis=0,...  6.32 us
    unnamed x16, local copies, waits for them, and re-layouts  4.45 us
  transfers between devices with their start and end apart: 3, of which 2 were waited for; matrix products, arithmetic and copies ran while one was open for 1% of the time, Pallas kernels for 21%

profile of v2, /device:TPU:12, one launch (start us, length us, event | category | flops | bytes accessed | tf_op | source)
XLA Modules:
  0.0 202.8 jit_solution(15521781949566369816)
XLA Ops:
  6.5 0.0 all-gather.2.cloned.1.call-start
  6.5 1.1 copy.12
  7.7 0.0 copy-start.6
  7.7 1.3 copy.13
  9.0 0.2 copy.14
  9.2 18.5 %all_to_all.20 = bf16[8,128,256]{2,1,0:T(8,128)(2,1)} all-to-all(bf16[8,128,256]{2,1,0:T(8,128)(2,1)S(1)} %copy.14), channel_id=1, replica_groups=mesh['blk'=16,'head'=8] {'head'}, dimensions={0} | all-to-all | bytes 1048576 | tf_op jit(solution)/shard_map/all_to_all | solution.py:190
  27.7 0.0 all-gather.2.cloned.1.call-update
  27.7 1.6 copy.19
  29.3 3.6 %all-to-all-start = ((bf16[8,128,1024]{2,1,0:T(8,128)(2,1)}), bf16[8,128,1024]{2,1,0:T(8,128)(2,1)S(1)}, u32[]{:S(2)}, u32[]{:S(2)}) async-start(bf16[8,128,1024]{2,1,0:T(8,128)(2,1)} %bitcast.24), calls=%async_computation | async-start | bytes 4194304 | tf_op jit(solution)/shard_map/all_to_all | solution.py:190
  32.9 8.2 %shard_map.55 = (s32[8,136]{1,0:T(8,128)}, s32[8,136]{1,0:T(8,128)}, s32[8]{0:T(128)}) custom-call(s32[1]{0:T(128)} %bitcast.shard_ref, s32[16,16,16]{2,1,0:T(8,128)} %codes_ref.1, s32[16,16]{1,0:T(8,128)} %counts_ref.1), custom_call_target="tpu_custom_call" | custom-call | bytes 20000000 | tf_op jit(solution)/shard_map/pallas_call | solution.py:63
  41.1 16.5 %all-to-all-done = bf16[8,128,1024]{2,1,0:T(8,128)(2,1)S(1)} async-done(((bf16[8,128,1024]{2,1,0:T(8,128)(2,1)}), bf16[8,128,1024]{2,1,0:T(8,128)(2,1)S(1)}, u32[]{:S(2)}, u32[]{:S(2)}) %all-to-all-start) | async-done | bytes 2097184 | tf_op jit(solution)/shard_map/all_to_all | solution.py:190
  57.6 37.5 %all-gather.2.cloned.1.call-done = bf16[16384,256]{1,0:T(8,128)(2,1)} async-done(((bf16[1024,256]{1,0:T(8,128)(2,1)}), bf16[16384,256]{1,0:T(8,128)(2,1)}) %all-gather.2.cloned.1.call-update) | async-done | bytes 8388624 | tf_op jit(solution)/shard_map/all_gather | solution.py:196
  95.1 0.7 copy-done
  95.8 0.7 copy-done.2
  96.5 0.7 copy-done.4
  97.1 35.1 %shard_map.57 = bf16[1024,512]{1,0:T(8,128)(2,1)} custom-call(s32[8,136]{1,0:T(8,128)S(1)} %copy-done, s32[8,136]{1,0:T(8,128)S(1)} %copy-done.2, s32[8]{0:T(128)S(1)} %copy-done.4, bf16[1024,1024]{1,0:T(8,128)(2,1)S(1)} %bitcast.21, bf16[128,128,256]{2,1,0:T(8,128)(2,1)} %bitcast.29), custom_call_target="tpu_custom_call" | custom-call | flops 18119393280 | bytes 12000000 | tf_op jit(solution)/shard_map/pallas_call | solution.py:159
  132.3 6.3 %all-to-all-start.3 = ((bf16[8,128,512]{2,1,0:T(8,128)(2,1)}), bf16[8,128,512]{2,1,0:T(8,128)(2,1)}, u32[]{:S(2)}, u32[]{:S(2)}) async-start(bf16[8,128,512]{2,1,0:T(8,128)(2,1)} %bitcast.9), calls=%async_computation.3 | async-start | bytes 2097152 | tf_op jit(solution)/shard_map/all_to_all | solution.py:206
  138.6 0.0 copy-done.3
  138.6 0.0 copy-done.5
  138.6 34.4 %shard_map.56 = bf16[1024,512]{1,0:T(8,128)(2,1)S(1)} custom-call(s32[8,136]{1,0:T(8,128)S(1)} %copy-done.1, s32[8,136]{1,0:T(8,128)S(1)} %copy-done.3, s32[8]{0:T(128)S(1)} %copy-done.5, bf16[1024,1024]{1,0:T(8,128)(2,1)S(1)} %bitcast.22, bf16[128,128,256]{2,1,0:T(8,128)(2,1)} %bitcast.30), custom_call_target="tpu_custom_call" | custom-call | flops 18119393280 | bytes 12000000 | tf_op jit(solution)/shard_map/pallas_call | solution.py:159
  173.0 0.0 all-to-all-done.3
  173.0 19.9 %all_to_all.21 = bf16[8,128,512]{2,1,0:T(8,128)(2,1)S(1)} all-to-all(bf16[8,128,512]{2,1,0:T(8,128)(2,1)S(1)} %bitcast.23), channel_id=1, replica_groups=mesh['blk'=16,'head'=8] {'head'}, dimensions={0} | all-to-all | bytes 2097152 | tf_op jit(solution)/shard_map/all_to_all | solution.py:206
  193.0 1.5 maximum_bitcast_fusion
  194.4 1.5 copy.17
  (9 shorter events, 0.1 us)
Async XLA Ops:
  6.5 88.5 %all-gather.2.cloned.1.call-start = ((), (), s32[]{:S(2)}) async-start(), calls=%async_computation.4 | async-start | bytes 8912896 | tf_op jit(solution)/shard_map/all_gather | solution.py:196
  7.7 20.1 %copy-start.6 = (bf16[128,8192]{1,0:T(8,128)(2,1)S(1)}, bf16[128,8192]{1,0:T(8,128)(2,1)}, u32[]{:S(2)}) copy-start(bf16[128,8192]{1,0:T(8,128)(2,1)} %param.5) | copy-start | bytes 6291460
  29.3 28.4 %all-to-all-start = ((bf16[8,128,1024]{2,1,0:T(8,128)(2,1)}), bf16[8,128,1024]{2,1,0:T(8,128)(2,1)S(1)}, u32[]{:S(2)}, u32[]{:S(2)}) async-start(bf16[8,128,1024]{2,1,0:T(8,128)(2,1)} %bitcast.24), calls=%async_computation | async-start | bytes 4194304 | tf_op jit(solution)/shard_map/all_to_all | solution.py:190
  95.1 0.7 copy-start
  95.8 0.7 copy-start.2
  96.5 0.7 copy-start.4
  132.2 6.3 %copy-start.1 = (s32[8,136]{1,0:T(8,128)S(1)}, s32[8,136]{1,0:T(8,128)}, u32[]{:S(2)}) copy-start(s32[8,136]{1,0:T(8,128)} %get-tuple-element.8.key_at) | copy-start | bytes 13060
  132.2 6.3 %copy-start.3 = (s32[8,136]{1,0:T(8,128)S(1)}, s32[8,136]{1,0:T(8,128)}, u32[]{:S(2)}) copy-start(s32[8,136]{1,0:T(8,128)} %get-tuple-element.9.value_at) | copy-start | bytes 13060
  132.2 6.3 %copy-start.5 = (s32[8]{0:T(128)S(1)}, s32[8]{0:T(128)}, u32[]{:S(2)}) copy-start(s32[8]{0:T(128)} %get-tuple-element.10.chunks) | copy-start | bytes 100
  132.3 40.8 %all-to-all-start.3 = ((bf16[8,128,512]{2,1,0:T(8,128)(2,1)}), bf16[8,128,512]{2,1,0:T(8,128)(2,1)}, u32[]{:S(2)}, u32[]{:S(2)}) async-start(bf16[8,128,512]{2,1,0:T(8,128)(2,1)} %bitcast.9), calls=%async_computation.3 | async-start | bytes 2097152 | tf_op jit(solution)/shard_map/all_to_all | solution.py:206
Sparse Core Ops, SparseCore 0:
  27.8 67.2 all-gather.1
